TPU v7x, 32 devices: a whole 2x2x4 slice. The times are simulated.
32 devices in a mesh: groups: 2 (over x), dp: 16 (over z, y, core).
Axes of the slice: x: 2, y: 2, z: 4, core: 2. Of those that a mesh axis runs over, the one named last changes fastest.
Arguments:
- hidden: bfloat16 [32, 8192], P(('groups', 'dp')), parts along dimension 0, may hold values from -6 to 6
- query_weight: bfloat16 [8192, 8192], P(None, 'dp'), may hold values from -0.0625 to 0.0625
- output_weight: bfloat16 [8192, 8192], P(None, 'dp'), may hold values from -0.0625 to 0.0625
- adapter_down: bfloat16 [64, 2, 8192, 64], P('dp'), may hold values from -0.0625 to 0.0625
- adapter_up: bfloat16 [64, 2, 64, 8192], P('dp'), may hold values from -0.75 to 0.75
- kv_cache: bfloat16 [32, 2, 512, 1024], P(('groups', 'dp')), parts along dimension 0
- cache_lengths: int32 [32], P(('groups', 'dp')), parts along dimension 0, may hold values from 1 to 512, as said below
- row_variant: int32 [32], P('groups'), parts along dimension 0, may hold values from 0 to 63
- variant_slot: int32 [64], replicated, may hold values from 0 to 63, as said below
Outputs:
- attended: bfloat16 [32, 8192], P(('groups', 'dp')), parts along dimension 0
There are 2 independent parts, one for each index of `groups`. A program takes and returns all parts, laid end to end along the dimension named above; an argument that names none is the same for every part. Nothing has to cross between parts.
Inputs may be any that keep to these rules, and one draw needn't show every extreme that they name: `cache_lengths`: some row's length is 512. `variant_slot`: distinct slots; slot s is held by index s // 4 of dp. Slot 63 is always used.
All inputs are finite; a program needn't handle non-finite values.
Results may differ from a plain program's by a relative error of at most 0.02.
The roundings to bfloat16 on the way count: a program that leaves them out, or rounds other values in their place, can miss the bound.
Values may be sent and summed in bfloat16 or wider, within the bound.
A program may use at most 192 MiB of HBM per device.

v0:
```python
import math

import jax
import jax.numpy as jnp
from jax import lax
from jax.sharding import PartitionSpec as P

HEADS = 64
KVH = 8
HDIM = 128


def body(
    hidden,
    query_weight,
    output_weight,
    adapter_down,
    adapter_up,
    kv_cache,
    cache_lengths,
    row_variant,
    variant_slot,
):
    devices = lax.axis_size("dp")
    myself = lax.axis_index("dp")
    owned = adapter_down.shape[0]
    rank_size = adapter_down.shape[3]
    width = hidden.shape[1]
    rows_dev = hidden.shape[0]
    all_rows = rows_dev * devices
    row_slot = jnp.sum(
        jnp.where(
            row_variant[:, None] == jnp.arange(variant_slot.shape[0], dtype=jnp.int32)[None, :],
            variant_slot[None, :],
            0,
        ),
        axis=1,
    )
    my_slots = myself * owned + jnp.arange(owned, dtype=jnp.int32)

    def project(row_block, weight, target):
        col_count = weight.shape[1]
        shard_rows = lax.all_gather(row_block, "dp", axis=0, tiled=True)
        base_part = jnp.dot(shard_rows, weight, preferred_element_type=jnp.float32)
        lowered = jnp.einsum(
            "pd,sdr->psr", shard_rows, adapter_down[:, target], preferred_element_type=jnp.float32
        )
        owner_mask = (row_slot[:, None] == my_slots[None, :]).astype(jnp.float32)
        reduced = jnp.sum(lowered * owner_mask[:, :, None], axis=1)
        joined = jnp.concatenate([base_part, reduced], axis=1)
        base_cols = joined[:, :col_count].astype(jnp.bfloat16)
        reduced = joined[:, col_count:]
        codes = reduced.astype(jnp.bfloat16)
        picked = (row_slot[:, None] == my_slots[None, :]).astype(jnp.bfloat16)
        spread = (picked[:, :, None] * codes[:, None, :]).reshape(all_rows, owned * rank_size)
        deltas = jnp.dot(
            spread,
            adapter_up[:, target].reshape(owned * rank_size, width),
            preferred_element_type=jnp.float32,
        ).astype(jnp.bfloat16)
        arrived = lax.all_to_all(base_cols, "dp", split_axis=0, concat_axis=1, tiled=True)
        returned = lax.all_to_all(
            deltas.reshape(all_rows, 1, width), "dp", split_axis=0, concat_axis=1, tiled=True
        )
        summed = jnp.sum(returned, axis=1, dtype=jnp.float32)
        return (arrived.astype(jnp.float32) + summed).astype(jnp.bfloat16)

    queries = project(hidden, query_weight, 0)
    cache_len = kv_cache.shape[2]
    grouped = queries.reshape(rows_dev, KVH, HEADS // KVH, HDIM)
    key_rows = kv_cache[:, 0].reshape(rows_dev, cache_len, KVH, HDIM)
    value_rows = kv_cache[:, 1].reshape(rows_dev, cache_len, KVH, HDIM)
    scaling = 1.0 / math.sqrt(HDIM)
    scores = (
        jnp.einsum("rkgd,rckd->rkgc", grouped, key_rows, preferred_element_type=jnp.float32)
        * scaling
    )
    visible = (jnp.arange(cache_len, dtype=jnp.int32)[None, :] < cache_lengths[:, None])[
        :, None, None, :
    ]
    masked = jnp.where(visible, scores, -1e30)
    highest = jnp.max(masked, axis=-1, keepdims=True)
    expon = jnp.where(visible, jnp.exp(masked - highest), 0.0)
    probs = (expon / jnp.sum(expon, axis=-1, keepdims=True)).astype(jnp.bfloat16)
    mixed = jnp.einsum("rkgc,rckd->rkgd", probs, value_rows, preferred_element_type=jnp.float32)
    mixed = mixed.astype(jnp.bfloat16).reshape(rows_dev, width)
    return project(mixed, output_weight, 1)


def solution(mesh):
    return jax.shard_map(
        body,
        mesh=mesh,
        in_specs=(
            P(("groups", "dp"), None),
            P(None, "dp"),
            P(None, "dp"),
            P("dp", None, None, None),
            P("dp", None, None, None),
            P(("groups", "dp"), None, None, None),
            P(("groups", "dp")),
            P("groups"),
            P(),
        ),
        out_specs=P(("groups", "dp"), None),
        check_vma=False,
    )
```

profile of v0, /device:TPU:0, one launch (start us, length us, event | category | flops | bytes accessed | tf_op | source)
XLA Modules:
  0.0 120.0 jit_solution(2978057546842223552)
XLA Ops:
  0.0 24.8 %all-gather = bf16[16,1,8192]{2,1,0:T(2,128)(2,1)S(1)} all-gather(bf16[1,1,8192]{2,1,0:T(2,128)(2,1)} %bitcast.73), channel_id=1, replica_groups=mesh['groups'=2,'dp'=16] {'dp'}, dimensions={0}, use_global_device_ids=true | all-gather | bytes 278528 | tf_op jit(solution)/shard_map/all_gather | solution.py:43
  24.8 0.0 copy-start
  24.8 0.0 copy-start.1
  24.8 4.6 %fusion.25 = bf16[16,1,512]{2,0,1:T(8,128)(2,1)S(1)} fusion(bf16[8192,512]{1,0:T(8,128)(2,1)} %param.10, bf16[16,1,8192]{2,1,0:T(2,128)(2,1)S(1)} %all-gather), kind=kOutput, calls=%fused_computation.23 | convolution fusion | flops 134225920 | bytes 8667136 | tf_op jit(solution)/shard_map/dot_general | solution.py:44
  29.4 0.5 broadcast.79
  29.9 0.6 reduce.9
  30.5 0.6 reshape.249
  31.1 3.5 %all-to-all-start = ((bf16[16,2,256]{2,1,0:T(2,128)(2,1)}), bf16[16,2,256]{2,1,0:T(2,128)(2,1)S(1)}, u32[]{:S(2)}, u32[]{:S(2)}) async-start(bf16[16,2,256]{2,1,0:T(2,128)(2,1)} %reshape.249), calls=%async_computation | async-start | bytes 32768 | tf_op jit(solution)/shard_map/all_to_all | solution.py:61
  34.6 0.0 copy-done
  34.6 0.0 copy-done.1
  34.6 0.2 select_reduce_fusion
  34.8 0.1 compare_convert_fusion.1
  34.9 0.1 copy.45
  35.0 3.9 %fusion.22 = bf16[16,64]{1,0:T(8,128)(2,1)S(1)} fusion(bf16[4,2,8192,64]{2,3,1,0:T(8,128)(2,1)} %param.12, bf16[16,1,8192]{2,1,0:T(2,128)(2,1)S(1)} %all-gather, f32[16,4]{0,1:T(4,128)S(1)} %get-tuple-element.10), kind=kOutput, calls=%fused_computation.22 | convolution fusion | flops 67116032 | bytes 4458752 | tf_op jit(solution)/shard_map/pd,sdr->psr/dot_general | solution.py:45
  38.9 0.1 broadcast_multiply_fusion.1
  39.0 0.1 mul.74
  39.1 5.2 %fusion.38 = (bf16[4,1,64,8192]{3,2,1,0:T(8,128)(2,1)}, bf16[4,1,64,8192]{3,2,1,0:T(8,128)(2,1)S(1)}) fusion(bf16[4,2,64,8192]{3,2,1,0:T(8,128)(2,1)} %param.13), kind=kLoop, calls=%fused_computation.49 | loop fusion | bytes 16777216 | tf_op jit(solution)/shard_map/slice | solution.py:58
  44.3 0.7 fusion.1
  45.0 0.7 reduce.8
  45.7 0.9 reshape.247
  46.6 0.0 all-to-all-done
  46.6 6.0 %all-to-all-start.1 = ((bf16[16,2,4096]{2,1,0:T(2,128)(2,1)}), bf16[16,2,4096]{2,1,0:T(2,128)(2,1)S(1)}, u32[]{:S(2)}, u32[]{:S(2)}) async-start(bf16[16,2,4096]{2,1,0:T(2,128)(2,1)} %reshape.247), calls=%async_computation.1 | async-start | bytes 524288 | tf_op jit(solution)/shard_map/all_to_all | solution.py:62
  53.2 1.7 %fusion.39 = (bf16[1,1,512,1024]{3,2,1,0:T(8,128)(2,1)S(1)}, bf16[1,1,512,1024]{3,2,1,0:T(8,128)(2,1)S(1)}) fusion(bf16[1,2,512,1024]{3,2,1,0:T(8,128)(2,1)} %param.14), kind=kLoop, calls=%fused_computation.50 | loop fusion | bytes 4194304 | tf_op jit(solution)/shard_map/slice | solution.py:71
  54.9 0.5 copy.62
  55.5 0.5 copy.63
  56.1 6.5 %all-to-all-done.1 = bf16[16,2,4096]{2,1,0:T(2,128)(2,1)S(1)} async-done(((bf16[16,2,4096]{2,1,0:T(2,128)(2,1)}), bf16[16,2,4096]{2,1,0:T(2,128)(2,1)S(1)}, u32[]{:S(2)}, u32[]{:S(2)}) %all-to-all-start.1) | async-done | bytes 262176 | tf_op jit(solution)/shard_map/all_to_all | solution.py:62
  62.6 0.3 reshape.248
  62.9 0.6 convert_reduce_fusion.1
  63.5 0.2 fusion.12
  63.7 0.2 fusion.40
  63.9 0.4 convolution_convert_fusion.3
  64.4 20.2 %all-gather.1 = bf16[16,1,8192]{2,1,0:T(2,128)(2,1)S(1)} all-gather(bf16[1,1,8192]{2,1,0:T(2,128)(2,1)S(1)} %reshape.240), channel_id=1, replica_groups=mesh['groups'=2,'dp'=16] {'dp'}, dimensions={0}, use_global_device_ids=true | all-gather | bytes 278528 | tf_op jit(solution)/shard_map/all_gather | solution.py:43
  84.6 3.9 %fusion.19 = bf16[16,64]{1,0:T(8,128)(2,1)S(1)} fusion(bf16[4,2,8192,64]{2,3,1,0:T(8,128)(2,1)} %param.12, bf16[16,1,8192]{2,1,0:T(2,128)(2,1)S(1)} %all-gather.1, f32[16,4]{0,1:T(4,128)S(1)} %get-tuple-element.10), kind=kOutput, calls=%fused_computation.21 | convolution fusion | flops 67116032 | bytes 4458752 | tf_op jit(solution)/shard_map/pd,sdr->psr/dot_general | solution.py:45
  88.5 0.1 broadcast_multiply_fusion
  88.6 0.1 mul.80
  88.7 4.6 %fusion.26 = bf16[16,1,512]{2,0,1:T(8,128)(2,1)S(1)} fusion(bf16[8192,512]{1,0:T(8,128)(2,1)} %param.11, bf16[16,1,8192]{2,1,0:T(2,128)(2,1)S(1)} %all-gather.1), kind=kOutput, calls=%fused_computation.24 | convolution fusion | flops 134225920 | bytes 8667136 | tf_op jit(solution)/shard_map/dot_general | solution.py:44
  93.3 0.6 reduce.11
  93.9 0.6 reshape.253
  94.5 3.5 %all-to-all-start.2 = ((bf16[16,2,256]{2,1,0:T(2,128)(2,1)}), bf16[16,2,256]{2,1,0:T(2,128)(2,1)S(1)}, u32[]{:S(2)}, u32[]{:S(2)}) async-start(bf16[16,2,256]{2,1,0:T(2,128)(2,1)} %reshape.253), calls=%async_computation.2 | async-start | bytes 32768 | tf_op jit(solution)/shard_map/all_to_all | solution.py:61
  98.0 2.8 %fusion.2 = bf16[16,1,8192]{2,0,1:T(8,128)(2,1)S(1)} fusion(bf16[16,256]{1,0:T(8,128)(2,1)S(1)} %mul.80, bf16[256,8192]{1,0:T(8,128)(2,1)} %bitcast.66), kind=kOutput, calls=%fused_computation.4 | convolution fusion | flops 67239936 | bytes 4464640 | tf_op jit(solution)/shard_map/dot_general | solution.py:56
  100.8 0.7 reduce.10
  101.6 0.9 reshape.251
  102.5 2.0 %all-to-all-done.2 = bf16[16,2,256]{2,1,0:T(2,128)(2,1)S(1)} async-done(((bf16[16,2,256]{2,1,0:T(2,128)(2,1)}), bf16[16,2,256]{2,1,0:T(2,128)(2,1)S(1)}, u32[]{:S(2)}, u32[]{:S(2)}) %all-to-all-start.2) | async-done | bytes 16416 | tf_op jit(solution)/shard_map/all_to_all | solution.py:61
  104.5 4.0 %all-to-all-start.3 = ((bf16[16,2,4096]{2,1,0:T(2,128)(2,1)}), bf16[16,2,4096]{2,1,0:T(2,128)(2,1)S(1)}, u32[]{:S(2)}, u32[]{:S(2)}) async-start(bf16[16,2,4096]{2,1,0:T(2,128)(2,1)} %reshape.251), calls=%async_computation.3 | async-start | bytes 524288 | tf_op jit(solution)/shard_map/all_to_all | solution.py:62
  108.5 10.0 %all-to-all-done.3 = bf16[16,2,4096]{2,1,0:T(2,128)(2,1)S(1)} async-done(((bf16[16,2,4096]{2,1,0:T(2,128)(2,1)}), bf16[16,2,4096]{2,1,0:T(2,128)(2,1)S(1)}, u32[]{:S(2)}, u32[]{:S(2)}) %all-to-all-start.3) | async-done | bytes 262176 | tf_op jit(solution)/shard_map/all_to_all | solution.py:62
  118.5 0.3 reshape.252
  118.8 0.6 convert_reduce_fusion
  119.4 0.7 fusion.36
  (7 shorter events, 0.1 us)
Async XLA Ops:
  24.8 9.9 %copy-start = (s32[64]{0:T(128)S(1)}, s32[64]{0:T(128)}, u32[]{:S(2)}) copy-start(s32[64]{0:T(128)} %param.17) | copy-start | bytes 772
  24.8 9.9 %copy-start.1 = (s32[16]{0:T(128)S(1)}, s32[16]{0:T(128)}, u32[]{:S(2)}) copy-start(s32[16]{0:T(128)} %param.16) | copy-start | bytes 196
  31.1 15.5 %all-to-all-start = ((bf16[16,2,256]{2,1,0:T(2,128)(2,1)}), bf16[16,2,256]{2,1,0:T(2,128)(2,1)S(1)}, u32[]{:S(2)}, u32[]{:S(2)}) async-start(bf16[16,2,256]{2,1,0:T(2,128)(2,1)} %reshape.249), calls=%async_computation | async-start | bytes 32768 | tf_op jit(solution)/shard_map/all_to_all | solution.py:61
  46.6 16.0 %all-to-all-start.1 = ((bf16[16,2,4096]{2,1,0:T(2,128)(2,1)}), bf16[16,2,4096]{2,1,0:T(2,128)(2,1)S(1)}, u32[]{:S(2)}, u32[]{:S(2)}) async-start(bf16[16,2,4096]{2,1,0:T(2,128)(2,1)} %reshape.247), calls=%async_computation.1 | async-start | bytes 524288 | tf_op jit(solution)/shard_map/all_to_all | solution.py:62
  94.5 10.0 %all-to-all-start.2 = ((bf16[16,2,256]{2,1,0:T(2,128)(2,1)}), bf16[16,2,256]{2,1,0:T(2,128)(2,1)S(1)}, u32[]{:S(2)}, u32[]{:S(2)}) async-start(bf16[16,2,256]{2,1,0:T(2,128)(2,1)} %reshape.253), calls=%async_computation.2 | async-start | bytes 32768 | tf_op jit(solution)/shard_map/all_to_all | solution.py:61
  104.5 14.0 %all-to-all-start.3 = ((bf16[16,2,4096]{2,1,0:T(2,128)(2,1)}), bf16[16,2,4096]{2,1,0:T(2,128)(2,1)S(1)}, u32[]{:S(2)}, u32[]{:S(2)}) async-start(bf16[16,2,4096]{2,1,0:T(2,128)(2,1)} %reshape.251), calls=%async_computation.3 | async-start | bytes 524288 | tf_op jit(solution)/shard_map/all_to_all | solution.py:62
where the time goes:
time: 121 us; the launch traced here: 120 us
  blocking collectives  45 us (37%)
  matrix products  21.2 us (18%)
  waiting for transfers between devices  18.5 us (15%)
  starting transfers between devices  16.9 us (14%)
  local copies, waits for them, and re-layouts  12.4 us (10%)
  other arithmetic  5.2 us (4%)
    all_gather x2, blocking collectives, project(): shard_rows = lax.all_gather(row_block, 'dp', axis=0, tiled=True)  45 us
    all_to_all x2, waiting for transfers between devices, project(): lax.all_to_all(deltas.reshape(all_rows, 1, width), 'dp', split_axis=0, co...  16.5 us
    all_to_all x2, starting transfers between devices, project(): lax.all_to_all(deltas.reshape(all_rows, 1, width), 'dp', split_axis=0, co...  9.95 us
    dot_general x2, matrix products, project(): base_part = jnp.dot(shard_rows, weight, preferred_element_type=jnp.float32)  9.17 us
    dot_general x2, matrix products, project(): jnp.einsum('pd,sdr->psr', shard_rows, adapter_down[:, target], preferred_...  7.84 us
    all_to_all x2, starting transfers between devices, project(): lax.all_to_all(base_cols, 'dp', split_axis=0, concat_axis=1, tiled=True)  6.99 us
    slice x1, local copies, waits for them, and re-layouts, project(): adapter_up[:, target].reshape(owned * rank_size, width)  5.19 us
    unnamed x15, local copies, waits for them, and re-layouts  4.66 us
  transfers between devices with their start and end apart: 4, of which 3 were waited for; matrix products, arithmetic and copies ran while one was open for 16% of the time, Pallas kernels for 0%

commit v1 on v0

--- a/solution.py
+++ b/solution.py
@@ -1,13 +1,422 @@
+import functools
 import math
 
 import jax
 import jax.numpy as jnp
 from jax import lax
+from jax.experimental import pallas as pl
+from jax.experimental.pallas import tpu as pltpu
 from jax.sharding import PartitionSpec as P
 
 HEADS = 64
 KVH = 8
 HDIM = 128
+GROUP = HEADS // KVH
+F32 = jnp.float32
+BF16 = jnp.bfloat16
+SCALING = 1.0 / math.sqrt(HDIM)
+MIB = 1 << 20
+NN = (((1,), (0,)), ((), ()))
+NT = (((1,), (1,)), ((), ()))
+
+
+def attention_kernel(
+    n,
+    variant_ref,
+    slots_ref,
+    length_ref,
+    hidden_ref,
+    wq_hbm,
+    wo_hbm,
+    down_hbm,
+    up_hbm,
+    kv_hbm,
+    out_ref,
+    weight,
+    down,
+    up,
+    kv,
+    gathered,
+    wide,
+    rows,
+    row32,
+    own_delta,
+    sibling_delta,
+    pair_delta,
+    delta_in,
+    base_out,
+    base_in,
+    local_sem,
+    gather_send,
+    gather_recv,
+    pair_send,
+    pair_recv,
+    delta_send,
+    delta_recv,
+    base_send,
+    base_recv,
+):
+    chips = n // 2
+    deep = chips // 2
+    owned = down_hbm.shape[0]
+    rank = down_hbm.shape[2]
+    width = down_hbm.shape[3]
+    cols = wq_hbm.shape[1]
+    blocks = cols // HDIM
+    me = lax.axis_index("dp")
+    core = lax.rem(me, 2)
+    chip = lax.div(me, 2)
+    y = lax.rem(chip, 2)
+    z = lax.div(chip, 2)
+    here = core * chips + chip
+
+    def copy_to(src, dst, send, recv, dev):
+        return pltpu.make_async_remote_copy(
+            src_ref=src,
+            dst_ref=dst,
+            send_sem=send,
+            recv_sem=recv,
+            device_id={"dp": dev},
+            device_id_type=pl.DeviceIdType.MESH,
+        )
+
+    depth = width // WPARTS
+    loads = {}
+    count = 0
+
+    def load(name, src, dst):
+        nonlocal count
+        copy = pltpu.make_async_copy(src, dst, local_sem.at[count])
+        count += 1
+        copy.start()
+        loads.setdefault(name, []).append(copy)
+
+    for phase, w_hbm in ((0, wq_hbm), (1, wo_hbm)):
+        for s in range(owned):
+            load(("down", phase), down_hbm.at[s, phase], down.at[phase, pl.ds(s * rank, rank)])
+        for s in range(owned):
+            load(("up", phase), up_hbm.at[s, phase], up.at[phase, pl.ds(s * rank, rank)])
+        for part in range(WPARTS):
+            cut = pl.ds(part * depth, depth)
+            load(("weight", phase, part), w_hbm.at[cut], weight.at[phase, cut])
+        if phase == 0:
+            load("kv", kv_hbm.at[0], kv)
+
+    def loaded(name):
+        for copy in loads[name]:
+            copy.wait()
+
+    for c in range(HEADS):
+        row32[pl.ds(c, 1), :] = hidden_ref[:, c * HDIM : (c + 1) * HDIM].astype(F32)
+
+    barrier = pltpu.get_barrier_semaphore()
+    for k in range(1, n):
+        pl.semaphore_signal(
+            barrier,
+            inc=1,
+            device_id={"dp": lax.rem(me + k, n)},
+            device_id_type=pl.DeviceIdType.MESH,
+        )
+
+    place = lax.broadcasted_iota(jnp.int32, (n, owned * rank), 0)
+    lane_slot = me * owned + lax.div(
+        lax.broadcasted_iota(jnp.int32, (n, owned * rank), 1), rank
+    )
+    row_slot = jnp.zeros((n, owned * rank), jnp.int32)
+    for p in range(n):
+        row = (p % chips) * 2 + p // chips
+        row_slot = jnp.where(place == p, slots_ref[variant_ref[row]], row_slot)
+    mine = row_slot == lane_slot
+
+    pl.semaphore_wait(barrier, n - 1)
+
+    def block(ref, phase, p):
+        return ref.at[phase, pl.ds(pl.multiple_of(p * HEADS, HEADS), HEADS)]
+
+    def project(phase):
+        sibling = me + 1 - 2 * core
+        across = (z * 2 + 1 - y) * 2 + core
+        waits = []
+
+        def send_row(p, dev, s):
+            ref = block(gathered, phase, p)
+            copy = copy_to(ref, ref, gather_send.at[phase, s], gather_recv.at[phase, p], dev)
+            copy.start()
+            waits.append(copy)
+
+        def arrived(p):
+            ref = block(gathered, phase, p)
+            copy_to(ref, ref, gather_send.at[phase, 0], gather_recv.at[phase, p], me).wait_recv()
+
+        gathered[phase, pl.ds(pl.multiple_of(here * HEADS, HEADS), HEADS), :] = row32[
+            ...
+        ].astype(BF16)
+        s = 0
+        for k in range(1, deep):
+            zz = lax.rem(z + k, deep)
+            send_row(here, (zz * 2 + y) * 2 + core, s)
+            s += 1
+        send_row(here, across, s)
+        send_row(here, sibling, s + 1)
+        s += 2
+        for k in range(1, deep):
+            zz = lax.rem(z + deep - k, deep)
+            p = core * chips + zz * 2 + y
+            arrived(p)
+            send_row(p, across, s)
+            send_row(p, sibling, s + 1)
+            s += 2
+        for k in range(deep):
+            zz = lax.rem(z + deep - k, deep)
+            p = core * chips + zz * 2 + 1 - y
+            arrived(p)
+            send_row(p, sibling, s)
+            s += 1
+        for k in range(chips):
+            arrived((1 - core) * chips + k)
+
+        wide[...] = gathered[phase].astype(F32)
+        for c in range(HEADS):
+            rows[:, c * HDIM : (c + 1) * HDIM] = wide[pl.ds(c, n, stride=HEADS), :].astype(BF16)
+
+        loaded(("down", phase))
+
+        def lower(k, acc):
+            cut = pl.ds(pl.multiple_of(k * KSTEP, KSTEP), KSTEP)
+            return acc + lax.dot_general(
+                rows[:, cut], down[phase, :, cut], NT, preferred_element_type=F32
+            )
+
+        low = lax.fori_loop(0, width // KSTEP, lower, jnp.zeros((n, owned * rank), F32))
+        codes = jnp.where(mine, low, 0.0).astype(BF16)
+        loaded(("up", phase))
+
+        def raise_(k, carry):
+            cut = pl.ds(pl.multiple_of(k * NSTEP, NSTEP), NSTEP)
+            term = lax.dot_general(codes, up[phase, :, cut], NN, preferred_element_type=F32)
+            for j in range(NSTEP // HDIM):
+                wide[pl.ds(k * (NSTEP // HDIM) + j, n, stride=HEADS), :] = term[
+                    :, j * HDIM : (j + 1) * HDIM
+                ]
+            return carry
+
+        lax.fori_loop(0, width // NSTEP, raise_, 0)
+        own_delta[phase] = wide[...].astype(BF16)
+        half = chips * HEADS
+        to_pair = copy_to(
+            own_delta.at[phase, pl.ds(pl.multiple_of((1 - core) * half, half), half)],
+            sibling_delta.at[phase],
+            pair_send.at[phase],
+            pair_recv.at[phase],
+            sibling,
+        )
+        to_pair.start()
+
+        def base_part(part, acc):
+            loaded(("weight", phase, part))
+
+            def step(k, acc):
+                cut = pl.ds(pl.multiple_of(part * depth + k * KSTEP, KSTEP), KSTEP)
+                return acc + lax.dot_general(
+                    rows[:, cut], weight[phase, cut, :], NN, preferred_element_type=F32
+                )
+
+            return lax.fori_loop(0, depth // KSTEP, step, acc)
+
+        acc = base_part(0, jnp.zeros((n, cols), F32))
+
+        to_pair.wait_recv()
+        pair_delta[phase] = (
+            own_delta[phase, pl.ds(pl.multiple_of(core * half, half), half), :].astype(F32)
+            + sibling_delta[phase].astype(F32)
+        ).astype(BF16)
+        for k in range(1, chips):
+            other = lax.rem(chip + k, chips)
+            copy = copy_to(
+                block(pair_delta, phase, other),
+                block(delta_in, phase, chip),
+                delta_send.at[phase, k],
+                delta_recv.at[phase, chip],
+                other * 2 + core,
+            )
+            copy.start()
+            waits.append(copy)
+
+        for part in range(1, WPARTS):
+            acc = base_part(part, acc)
+        acc = acc.astype(BF16).astype(F32)
+        for j in range(blocks):
+            base_out[phase, pl.ds(j, n, stride=8), :] = acc[:, j * HDIM : (j + 1) * HDIM]
+
+        def part_of(ref, p):
+            return ref.at[phase, pl.ds(pl.multiple_of(p * 8, 8), 8)]
+
+        for k in range(1, n):
+            dev = lax.rem(me + k, n)
+            p = lax.rem(dev, 2) * chips + lax.div(dev, 2)
+            copy = copy_to(
+                part_of(base_out, p),
+                part_of(base_in, me),
+                base_send.at[phase, k],
+                base_recv.at[phase, me],
+                dev,
+            )
+            copy.start()
+            waits.append(copy)
+        base_in[phase, pl.ds(pl.multiple_of(me * 8, 8), 8), :] = base_out[
+            phase, pl.ds(pl.multiple_of(here * 8, 8), 8), :
+        ]
+
+        total = pair_delta[
+            phase, pl.ds(pl.multiple_of(chip * HEADS, HEADS), HEADS), :
+        ].astype(F32)
+        for k in range(1, chips):
+            other = lax.rem(chip + chips - k, chips)
+            ref = block(delta_in, phase, other)
+            copy_to(
+                ref, ref, delta_send.at[phase, 0], delta_recv.at[phase, other], me
+            ).wait_recv()
+            total = total + delta_in[
+                phase, pl.ds(pl.multiple_of(other * HEADS, HEADS), HEADS), :
+            ].astype(F32)
+        for k in range(1, n):
+            src = lax.rem(me + n - k, n)
+            ref = part_of(base_in, src)
+            copy_to(ref, ref, base_send.at[phase, 0], base_recv.at[phase, src], me).wait_recv()
+        for src in range(n):
+            row32[pl.ds(src * blocks, blocks), :] = base_in[phase, pl.ds(src * 8, blocks), :]
+        result = (row32[...] + total).astype(BF16)
+        to_pair.wait_send()
+        for copy in waits:
+            copy.wait_send()
+        return result
+
+    row32[...] = project(0).astype(F32)
+
+    loaded("kv")
+    cache_len = kv.shape[1]
+    length = length_ref[0]
+    scores = []
+    for g in range(KVH):
+        q = row32[pl.ds(g * GROUP, GROUP), :].astype(BF16)
+        scores.append(
+            lax.dot_general(
+                q, kv[0, :, g * HDIM : (g + 1) * HDIM], NT, preferred_element_type=F32
+            )
+        )
+    scores = jnp.concatenate(scores, axis=0) * SCALING
+    visible = lax.broadcasted_iota(jnp.int32, (HEADS, cache_len), 1) < length
+    masked = jnp.where(visible, scores, -1e30)
+    highest = jnp.max(masked, axis=-1, keepdims=True)
+    expon = jnp.where(visible, jnp.exp(masked - highest), 0.0)
+    probs = expon / jnp.sum(expon, axis=-1, keepdims=True)
+    for g in range(KVH):
+        row32[pl.ds(g * GROUP, GROUP), :] = lax.dot_general(
+            probs[g * GROUP : (g + 1) * GROUP].astype(BF16),
+            kv[1, :, g * HDIM : (g + 1) * HDIM],
+            NN,
+            preferred_element_type=F32,
+        )
+
+    out_ref[...] = project(1)
+
+
+WPARTS = 4
+KSTEP = 1024
+NSTEP = 512
+
+
+def fused_body(
+    hidden,
+    query_weight,
+    output_weight,
+    adapter_down,
+    adapter_up,
+    kv_cache,
+    cache_lengths,
+    row_variant,
+    variant_slot,
+):
+    n = lax.axis_size("dp")
+    width = hidden.shape[1]
+    owned, _, _, rank = adapter_down.shape
+    cols = query_weight.shape[1]
+    chips = n // 2
+    smem = pl.BlockSpec(memory_space=pltpu.SMEM)
+    vmem = pl.BlockSpec(memory_space=pltpu.VMEM)
+    anywhere = pl.BlockSpec(memory_space=pl.ANY)
+    dma = pltpu.SemaphoreType.DMA
+    weights = width * (2 * cols + 4 * owned * rank)
+    macs = n * weights + 2 * HEADS * HDIM * kv_cache.shape[2]
+    out = pl.pallas_call(
+        functools.partial(attention_kernel, n),
+        out_shape=jax.ShapeDtypeStruct((HEADS, HDIM), BF16),
+        in_specs=[smem, smem, smem, vmem] + [anywhere] * 5,
+        out_specs=vmem,
+        scratch_shapes=[
+            pltpu.VMEM((2, width, cols), BF16),
+            pltpu.VMEM((2, owned * rank, width), BF16),
+            pltpu.VMEM((2, owned * rank, width), BF16),
+            pltpu.VMEM(kv_cache.shape[1:], BF16),
+            pltpu.VMEM((2, n * HEADS, HDIM), BF16),
+            pltpu.VMEM((n * HEADS, HDIM), F32),
+            pltpu.VMEM((n, width), BF16),
+            pltpu.VMEM((HEADS, HDIM), F32),
+            pltpu.VMEM((2, n * HEADS, HDIM), BF16),
+            pltpu.VMEM((2, chips * HEADS, HDIM), BF16),
+            pltpu.VMEM((2, chips * HEADS, HDIM), BF16),
+            pltpu.VMEM((2, chips * HEADS, HDIM), BF16),
+            pltpu.VMEM((2, n * 8, HDIM), F32),
+            pltpu.VMEM((2, n * 8, HDIM), F32),
+            dma((4 * owned + 2 * WPARTS + 1,)),
+            dma((2, n)),
+            dma((2, n)),
+            dma((2,)),
+            dma((2,)),
+            dma((2, chips)),
+            dma((2, chips)),
+            dma((2, n)),
+            dma((2, n)),
+        ],
+        compiler_params=pltpu.CompilerParams(
+            collective_id=0, has_side_effects=True, vmem_limit_bytes=52 * MIB
+        ),
+        cost_estimate=pl.CostEstimate(
+            flops=2 * macs,
+            bytes_accessed=2 * (weights + kv_cache.size),
+            transcendentals=HEADS * kv_cache.shape[2],
+        ),
+        name="adapter_attention",
+    )(
+        row_variant,
+        variant_slot,
+        cache_lengths,
+        hidden,
+        query_weight,
+        output_weight,
+        jnp.swapaxes(adapter_down, 2, 3),
+        adapter_up,
+        kv_cache,
+    )
+    return out.reshape(1, width)
+
+
+def fits(mesh, hidden, query_weight, adapter_down, kv_cache):
+    n = mesh.shape["dp"]
+    cols = query_weight.shape[1] // n
+    width = hidden.shape[1]
+    owned = adapter_down.shape[0] // n
+    held = 4 * width * cols + 8 * owned * adapter_down.shape[3] * width
+    held += 2 * kv_cache.size // kv_cache.shape[0]
+    return (
+        hidden.shape[0] == n * mesh.shape["groups"]
+        and width == HEADS * HDIM
+        and n % 16 == 0
+        and n <= 32
+        and cols % HDIM == 0
+        and cols <= 8 * HDIM
+        and held <= 40 * MIB
+    )
 
 
 def body(
@@ -88,20 +497,26 @@
 
 
 def solution(mesh):
-    return jax.shard_map(
-        body,
-        mesh=mesh,
-        in_specs=(
-            P(("groups", "dp"), None),
-            P(None, "dp"),
-            P(None, "dp"),
-            P("dp", None, None, None),
-            P("dp", None, None, None),
-            P(("groups", "dp"), None, None, None),
-            P(("groups", "dp")),
-            P("groups"),
-            P(),
-        ),
-        out_specs=P(("groups", "dp"), None),
-        check_vma=False,
+    in_specs = (
+        P(("groups", "dp"), None),
+        P(None, "dp"),
+        P(None, "dp"),
+        P("dp", None, None, None),
+        P("dp", None, None, None),
+        P(("groups", "dp"), None, None, None),
+        P(("groups", "dp")),
+        P("groups"),
+        P(),
     )
+
+    def run(*args):
+        fused = fits(mesh, args[0], args[1], args[3], args[5])
+        return jax.shard_map(
+            fused_body if fused else body,
+            mesh=mesh,
+            in_specs=in_specs,
+            out_specs=P(("groups", "dp"), None),
+            check_vma=False,
+        )(*args)
+
+    return run

time: 121 us -> 52.7 us (0.44)
  Pallas kernels: 0 us -> 49.1 us
  blocking collectives: 45 us -> 0 us
  matrix products: 21.2 us -> 0 us
  waiting for transfers between devices: 18.5 us -> 0 us
  starting transfers between devices: 16.9 us -> 0 us
  local copies, waits for them, and re-layouts: 12.4 us -> 2.7 us
  other arithmetic: 5.2 us -> 0 us
    pallas_call x0 -> x1, Pallas kernels: none -> 49.1 us  [fused_body(): pl.pallas_call(functools.partial(attention_kernel, n), out_shape=jax.Shap...]
    all_gather x2 -> x0, blocking collectives: 45 us -> none  [project(): shard_rows = lax.all_gather(row_block, 'dp', axis=0, tiled=True)]
    dot_general x8 -> x0, matrix products: 21.2 us -> none  [the longest x2 9.17 us: project(): base_part = jnp.dot(shard_rows, weight, preferred_element_type=jnp.float32)]
    all_to_all x4 -> x0, waiting for transfers between devices: 18.5 us -> none  [the longest x2 16.5 us: project(): lax.all_to_all(deltas.reshape(all_rows, 1, width), 'dp', split_axis=0, co...]
    all_to_all x4 -> x0, starting transfers between devices: 16.9 us -> none  [the longest x2 9.95 us: project(): lax.all_to_all(deltas.reshape(all_rows, 1, width), 'dp', split_axis=0, co...]
    slice x2 -> x0, local copies, waits for them, and re-layouts: 6.91 us -> none  [the longest x1 5.19 us: project(): adapter_up[:, target].reshape(owned * rank_size, width)]
    unnamed x15 -> x7, local copies, waits for them, and re-layouts: 4.66 us -> 2.7 us
    reshape x2 -> x0, other arithmetic: 1.5 us -> none  [project(): deltas.reshape(all_rows, 1, width)]
  transfers between devices with their start and end apart: 4 -> 0, of which waited for: 3 -> 0; matrix products, arithmetic and copies ran while one was open for 16% -> 0% of each run, Pallas kernels for 0% -> 0%
where the time goes in v1:
time: 52.7 us; the launch traced here: 52.5 us
  Pallas kernels  49.1 us (93%)
  local copies, waits for them, and re-layouts  2.7 us (5%)
  between operations  0.67 us (1%)
    pallas_call x1, Pallas kernels, fused_body(): pl.pallas_call(functools.partial(attention_kernel, n), out_shape=jax.Shap...  49.1 us
    unnamed x7, local copies, waits for them, and re-layouts  2.7 us

profile of v1, /device:TPU:0, one launch (start us, length us, event | category | flops | bytes accessed | tf_op | source)
XLA Modules:
  0.0 52.5 jit_solution(15411836388679396945)
XLA Ops:
  0.7 0.0 copy-start
  0.7 0.7 %copy-done = bf16[1,8192]{1,0:T(2,128)(2,1)S(1)} copy-done((bf16[1,8192]{1,0:T(2,128)(2,1)S(1)}, bf16[1,8192]{1,0:T(2,128)(2,1)}, u32[]{:S(2)}) %copy-start) | copy-done | bytes 16408
  1.4 0.0 copy-start.1
  1.4 0.7 %copy-done.1 = s32[16]{0:T(128)S(1)} copy-done((s32[16]{0:T(128)S(1)}, s32[16]{0:T(128)}, u32[]{:S(2)}) %copy-start.1) | copy-done | bytes 88
  2.1 0.0 copy-start.2
  2.1 0.7 %copy-done.2 = s32[64]{0:T(128)S(1)} copy-done((s32[64]{0:T(128)S(1)}, s32[64]{0:T(128)}, u32[]{:S(2)}) %copy-start.2) | copy-done | bytes 280
  2.7 49.1 %adapter_attention.1 = bf16[64,128]{1,0:T(8,128)(2,1)S(1)} custom-call(s32[16]{0:T(128)S(1)} %copy-done.1, s32[64]{0:T(128)S(1)} %copy-done.2, s32[1]{0:T(128)S(6)} %copy.13.length_ref, bf16[1,8192]{1,0:T(2,128)(2,1)S(1)} %copy-done, bf16[8192,512]{1,0:T(8,128)(2,1)} %wq_hbm.1, bf16[8192,512]{1,0:T(8,128)(2,1)} %wo_hbm.1, bf16[4,2,64,8192]{3,2,1,0:T(8,128)(2,1)} %bitcast.7, ...), custom_call_target="tpu_custom_call" | custom-call | flops 553648128 | bytes 35651584 | tf_op jit(solution)/shard_map/adapter_attention/pallas_call | solution.py:351
  51.8 0.6 %copy.12 = bf16[1,1,64,128]{3,1,2,0:T(2,128)(2,1)} copy(bf16[1,1,64,128]{3,2,1,0:T(8,128)(2,1)S(1)} %bitcast.6) | data formatting | bytes 32768
Async XLA Ops:
  0.7 0.8 %copy-start = (bf16[1,8192]{1,0:T(2,128)(2,1)S(1)}, bf16[1,8192]{1,0:T(2,128)(2,1)}, u32[]{:S(2)}) copy-start(bf16[1,8192]{1,0:T(2,128)(2,1)} %hidden_ref.1) | copy-start | bytes 49156
  1.4 0.7 %copy-start.1 = (s32[16]{0:T(128)S(1)}, s32[16]{0:T(128)}, u32[]{:S(2)}) copy-start(s32[16]{0:T(128)} %variant_ref.1) | copy-start | bytes 196
  2.1 0.7 %copy-start.2 = (s32[64]{0:T(128)S(1)}, s32[64]{0:T(128)}, u32[]{:S(2)}) copy-start(s32[64]{0:T(128)} %slots_ref.1) | copy-start | bytes 772

commit v2 on v1

--- a/solution.py
+++ b/solution.py
@@ -12,6 +12,7 @@
 KVH = 8
 HDIM = 128
 GROUP = HEADS // KVH
+HALF = HEADS // 2
 F32 = jnp.float32
 BF16 = jnp.bfloat16
 SCALING = 1.0 / math.sqrt(HDIM)
@@ -22,16 +23,20 @@
 
 def attention_kernel(
     n,
-    variant_ref,
-    slots_ref,
-    length_ref,
-    hidden_ref,
+    variant_hbm,
+    slots_hbm,
+    length_hbm,
+    hidden_hbm,
     wq_hbm,
     wo_hbm,
     down_hbm,
     up_hbm,
     kv_hbm,
     out_ref,
+    variant_ref,
+    slots_ref,
+    length_ref,
+    hidden_ref,
     weight,
     down,
     up,
@@ -57,7 +62,6 @@
     base_recv,
 ):
     chips = n // 2
-    deep = chips // 2
     owned = down_hbm.shape[0]
     rank = down_hbm.shape[2]
     width = down_hbm.shape[3]
@@ -66,8 +70,6 @@
     me = lax.axis_index("dp")
     core = lax.rem(me, 2)
     chip = lax.div(me, 2)
-    y = lax.rem(chip, 2)
-    z = lax.div(chip, 2)
     here = core * chips + chip
 
     def copy_to(src, dst, send, recv, dev):
@@ -91,6 +93,10 @@
         copy.start()
         loads.setdefault(name, []).append(copy)
 
+    load("hidden", hidden_hbm, hidden_ref)
+    load("variant", variant_hbm, variant_ref)
+    load("slots", slots_hbm, slots_ref)
+    load("length", length_hbm, length_ref)
     for phase, w_hbm in ((0, wq_hbm), (1, wo_hbm)):
         for s in range(owned):
             load(("down", phase), down_hbm.at[s, phase], down.at[phase, pl.ds(s * rank, rank)])
@@ -106,9 +112,6 @@
         for copy in loads[name]:
             copy.wait()
 
-    for c in range(HEADS):
-        row32[pl.ds(c, 1), :] = hidden_ref[:, c * HDIM : (c + 1) * HDIM].astype(F32)
-
     barrier = pltpu.get_barrier_semaphore()
     for k in range(1, n):
         pl.semaphore_signal(
@@ -117,6 +120,14 @@
             device_id={"dp": lax.rem(me + k, n)},
             device_id_type=pl.DeviceIdType.MESH,
         )
+
+    loaded("hidden")
+    for c in range(HEADS):
+        row32[pl.ds(c, 1), :] = hidden_ref[:, c * HDIM : (c + 1) * HDIM].astype(F32)
+
+    loaded("variant")
+    loaded("slots")
+    loaded("length")
 
     place = lax.broadcasted_iota(jnp.int32, (n, owned * rank), 0)
     lane_slot = me * owned + lax.div(
@@ -135,7 +146,6 @@
 
     def project(phase):
         sibling = me + 1 - 2 * core
-        across = (z * 2 + 1 - y) * 2 + core
         waits = []
 
         def send_row(p, dev, s):
@@ -151,27 +161,13 @@
         gathered[phase, pl.ds(pl.multiple_of(here * HEADS, HEADS), HEADS), :] = row32[
             ...
         ].astype(BF16)
-        s = 0
-        for k in range(1, deep):
-            zz = lax.rem(z + k, deep)
-            send_row(here, (zz * 2 + y) * 2 + core, s)
-            s += 1
-        send_row(here, across, s)
-        send_row(here, sibling, s + 1)
-        s += 2
-        for k in range(1, deep):
-            zz = lax.rem(z + deep - k, deep)
-            p = core * chips + zz * 2 + y
+        for k in range(1, chips):
+            send_row(here, lax.rem(chip + k, chips) * 2 + core, k)
+        send_row(here, sibling, 0)
+        for k in range(1, chips):
+            p = core * chips + lax.rem(chip + chips - k, chips)
             arrived(p)
-            send_row(p, across, s)
-            send_row(p, sibling, s + 1)
-            s += 2
-        for k in range(deep):
-            zz = lax.rem(z + deep - k, deep)
-            p = core * chips + zz * 2 + 1 - y
-            arrived(p)
-            send_row(p, sibling, s)
-            s += 1
+            send_row(p, sibling, chips + k)
         for k in range(chips):
             arrived((1 - core) * chips + k)
 
@@ -181,68 +177,79 @@
 
         loaded(("down", phase))
 
-        def lower(k, acc):
-            cut = pl.ds(pl.multiple_of(k * KSTEP, KSTEP), KSTEP)
-            return acc + lax.dot_general(
-                rows[:, cut], down[phase, :, cut], NT, preferred_element_type=F32
-            )
-
-        low = lax.fori_loop(0, width // KSTEP, lower, jnp.zeros((n, owned * rank), F32))
+        low = lax.dot_general(
+            down[phase], rows[...], NT, preferred_element_type=F32
+        ).T
         codes = jnp.where(mine, low, 0.0).astype(BF16)
         loaded(("up", phase))
 
-        def raise_(k, carry):
-            cut = pl.ds(pl.multiple_of(k * NSTEP, NSTEP), NSTEP)
+        def raise_(k):
+            cut = pl.ds(k * NSTEP, NSTEP)
             term = lax.dot_general(codes, up[phase, :, cut], NN, preferred_element_type=F32)
+            first = k * (NSTEP // HDIM)
+            half = first // HALF
+            first = first - half * HALF + half * (n * HALF)
             for j in range(NSTEP // HDIM):
-                wide[pl.ds(k * (NSTEP // HDIM) + j, n, stride=HEADS), :] = term[
-                    :, j * HDIM : (j + 1) * HDIM
-                ]
-            return carry
-
-        lax.fori_loop(0, width // NSTEP, raise_, 0)
-        own_delta[phase] = wide[...].astype(BF16)
-        half = chips * HEADS
-        to_pair = copy_to(
-            own_delta.at[phase, pl.ds(pl.multiple_of((1 - core) * half, half), half)],
-            sibling_delta.at[phase],
-            pair_send.at[phase],
-            pair_recv.at[phase],
-            sibling,
-        )
-        to_pair.start()
+                wide[pl.ds(first + j, n, stride=HALF), :] = term[:, j * HDIM : (j + 1) * HDIM]
+
+        side = chips * HALF
+        to_pair = []
+        for half in (0, 1):
+            steps = width // NSTEP // 2
+            for k in range(half * steps, (half + 1) * steps):
+                raise_(k)
+            own_delta[phase, half] = wide[half * n * HALF : (half + 1) * n * HALF, :].astype(BF16)
+            copy = copy_to(
+                own_delta.at[
+                    phase, half, pl.ds(pl.multiple_of((1 - core) * side, side), side)
+                ],
+                sibling_delta.at[phase, half],
+                pair_send.at[phase, half],
+                pair_recv.at[phase, half],
+                sibling,
+            )
+            copy.start()
+            to_pair.append(copy)
+            waits.append(copy)
+
+        def piece(ref, half, c):
+            return ref.at[phase, half, pl.ds(pl.multiple_of(c * HALF, HALF), HALF)]
+
+        def forward(half):
+            to_pair[half].wait_recv()
+            pair_delta[phase, half] = (
+                own_delta[
+                    phase, half, pl.ds(pl.multiple_of(core * side, side), side), :
+                ].astype(F32)
+                + sibling_delta[phase, half].astype(F32)
+            ).astype(BF16)
+            for k in range(1, chips):
+                other = lax.rem(chip + k, chips)
+                copy = copy_to(
+                    piece(pair_delta, half, other),
+                    piece(delta_in, half, chip),
+                    delta_send.at[phase, half, k],
+                    delta_recv.at[phase, half, chip],
+                    other * 2 + core,
+                )
+                copy.start()
+                waits.append(copy)
+
+        forward(0)
 
         def base_part(part, acc):
             loaded(("weight", phase, part))
 
-            def step(k, acc):
-                cut = pl.ds(pl.multiple_of(part * depth + k * KSTEP, KSTEP), KSTEP)
-                return acc + lax.dot_general(
-                    rows[:, cut], weight[phase, cut, :], NN, preferred_element_type=F32
-                )
-
-            return lax.fori_loop(0, depth // KSTEP, step, acc)
-
-        acc = base_part(0, jnp.zeros((n, cols), F32))
-
-        to_pair.wait_recv()
-        pair_delta[phase] = (
-            own_delta[phase, pl.ds(pl.multiple_of(core * half, half), half), :].astype(F32)
-            + sibling_delta[phase].astype(F32)
-        ).astype(BF16)
-        for k in range(1, chips):
-            other = lax.rem(chip + k, chips)
-            copy = copy_to(
-                block(pair_delta, phase, other),
-                block(delta_in, phase, chip),
-                delta_send.at[phase, k],
-                delta_recv.at[phase, chip],
-                other * 2 + core,
+            cut = pl.ds(part * depth, depth)
+            return acc + lax.dot_general(
+                rows[:, cut], weight[phase, cut, :], NN, preferred_element_type=F32
             )
-            copy.start()
-            waits.append(copy)
-
-        for part in range(1, WPARTS):
+
+        acc = jnp.zeros((n, cols), F32)
+        for part in range(WPARTS // 2):
+            acc = base_part(part, acc)
+        forward(1)
+        for part in range(WPARTS // 2, WPARTS):
             acc = base_part(part, acc)
         acc = acc.astype(BF16).astype(F32)
         for j in range(blocks):
@@ -267,18 +274,22 @@
             phase, pl.ds(pl.multiple_of(here * 8, 8), 8), :
         ]
 
-        total = pair_delta[
-            phase, pl.ds(pl.multiple_of(chip * HEADS, HEADS), HEADS), :
-        ].astype(F32)
-        for k in range(1, chips):
-            other = lax.rem(chip + chips - k, chips)
-            ref = block(delta_in, phase, other)
-            copy_to(
-                ref, ref, delta_send.at[phase, 0], delta_recv.at[phase, other], me
-            ).wait_recv()
-            total = total + delta_in[
-                phase, pl.ds(pl.multiple_of(other * HEADS, HEADS), HEADS), :
+        totals = []
+        for half in (0, 1):
+            total = pair_delta[
+                phase, half, pl.ds(pl.multiple_of(chip * HALF, HALF), HALF), :
             ].astype(F32)
+            for k in range(1, chips):
+                other = lax.rem(chip + chips - k, chips)
+                ref = piece(delta_in, half, other)
+                copy_to(
+                    ref, ref, delta_send.at[phase, half, 0], delta_recv.at[phase, half, other], me
+                ).wait_recv()
+                total = total + delta_in[
+                    phase, half, pl.ds(pl.multiple_of(other * HALF, HALF), HALF), :
+                ].astype(F32)
+            totals.append(total)
+        total = jnp.concatenate(totals, axis=0)
         for k in range(1, n):
             src = lax.rem(me + n - k, n)
             ref = part_of(base_in, src)
@@ -286,7 +297,6 @@
         for src in range(n):
             row32[pl.ds(src * blocks, blocks), :] = base_in[phase, pl.ds(src * 8, blocks), :]
         result = (row32[...] + total).astype(BF16)
-        to_pair.wait_send()
         for copy in waits:
             copy.wait_send()
         return result
@@ -322,7 +332,6 @@
 
 
 WPARTS = 4
-KSTEP = 1024
 NSTEP = 512
 
 
@@ -342,18 +351,21 @@
     owned, _, _, rank = adapter_down.shape
     cols = query_weight.shape[1]
     chips = n // 2
-    smem = pl.BlockSpec(memory_space=pltpu.SMEM)
     vmem = pl.BlockSpec(memory_space=pltpu.VMEM)
-    anywhere = pl.BlockSpec(memory_space=pl.ANY)
+    hbm = pl.BlockSpec(memory_space=pltpu.HBM)
     dma = pltpu.SemaphoreType.DMA
     weights = width * (2 * cols + 4 * owned * rank)
     macs = n * weights + 2 * HEADS * HDIM * kv_cache.shape[2]
     out = pl.pallas_call(
         functools.partial(attention_kernel, n),
         out_shape=jax.ShapeDtypeStruct((HEADS, HDIM), BF16),
-        in_specs=[smem, smem, smem, vmem] + [anywhere] * 5,
+        in_specs=[hbm] * 9,
         out_specs=vmem,
         scratch_shapes=[
+            pltpu.SMEM(row_variant.shape, jnp.int32),
+            pltpu.SMEM(variant_slot.shape, jnp.int32),
+            pltpu.SMEM(cache_lengths.shape, jnp.int32),
+            pltpu.VMEM(hidden.shape, BF16),
             pltpu.VMEM((2, width, cols), BF16),
             pltpu.VMEM((2, owned * rank, width), BF16),
             pltpu.VMEM((2, owned * rank, width), BF16),
@@ -362,24 +374,24 @@
             pltpu.VMEM((n * HEADS, HDIM), F32),
             pltpu.VMEM((n, width), BF16),
             pltpu.VMEM((HEADS, HDIM), F32),
-            pltpu.VMEM((2, n * HEADS, HDIM), BF16),
-            pltpu.VMEM((2, chips * HEADS, HDIM), BF16),
-            pltpu.VMEM((2, chips * HEADS, HDIM), BF16),
-            pltpu.VMEM((2, chips * HEADS, HDIM), BF16),
+            pltpu.VMEM((2, 2, n * HALF, HDIM), BF16),
+            pltpu.VMEM((2, 2, chips * HALF, HDIM), BF16),
+            pltpu.VMEM((2, 2, chips * HALF, HDIM), BF16),
+            pltpu.VMEM((2, 2, chips * HALF, HDIM), BF16),
             pltpu.VMEM((2, n * 8, HDIM), F32),
             pltpu.VMEM((2, n * 8, HDIM), F32),
-            dma((4 * owned + 2 * WPARTS + 1,)),
+            dma((4 * owned + 2 * WPARTS + 5,)),
             dma((2, n)),
             dma((2, n)),
-            dma((2,)),
-            dma((2,)),
-            dma((2, chips)),
-            dma((2, chips)),
+            dma((2, 2)),
+            dma((2, 2)),
+            dma((2, 2, chips)),
+            dma((2, 2, chips)),
             dma((2, n)),
             dma((2, n)),
         ],
         compiler_params=pltpu.CompilerParams(
-            collective_id=0, has_side_effects=True, vmem_limit_bytes=52 * MIB
+            collective_id=0, has_side_effects=True, vmem_limit_bytes=63 * MIB
         ),
         cost_estimate=pl.CostEstimate(
             flops=2 * macs,

time: 52.7 us -> 46.6 us (0.88)
  Pallas kernels: 49.1 us -> 44.3 us
  local copies, waits for them, and re-layouts: 2.7 us -> 1.36 us
    pallas_call x1, Pallas kernels: 49.1 us -> 44.3 us  [fused_body(): pl.pallas_call(functools.partial(attention_kernel, n), out_shape=jax.Shap...]
    unnamed x7 -> x1, local copies, waits for them, and re-layouts: 2.7 us -> 1.36 us
where the time goes in v2:
time: 46.6 us; the launch traced here: 46.3 us
  Pallas kernels  44.3 us (95%)
  local copies, waits for them, and re-layouts  1.36 us (3%)
  between operations  0.66 us (1%)
    pallas_call x1, Pallas kernels, fused_body(): pl.pallas_call(functools.partial(attention_kernel, n), out_shape=jax.Shap...  44.3 us
    unnamed x1, local copies, waits for them, and re-layouts  1.36 us

profile of v2, /device:TPU:0, one launch (start us, length us, event | category | flops | bytes accessed | tf_op | source)
XLA Modules:
  0.0 46.3 jit_solution(5794183872676491195)
XLA Ops:
  0.7 44.3 %adapter_attention.1 = bf16[64,128]{1,0:T(8,128)(2,1)} custom-call(s32[16]{0:T(128)} %variant_hbm.1, s32[64]{0:T(128)} %slots_hbm.1, s32[1]{0:T(128)S(6)} %copy.13.length_hbm, bf16[1,8192]{1,0:T(2,128)(2,1)} %hidden_hbm.1, bf16[8192,512]{1,0:T(8,128)(2,1)} %wq_hbm.1, bf16[8192,512]{1,0:T(8,128)(2,1)} %wo_hbm.1, bf16[4,2,64,8192]{3,2,1,0:T(8,128)(2,1)} %bitcast.6, ...), custom_call_target="tpu_custom_call" | custom-call | flops 553648128 | bytes 35651584 | tf_op jit(solution)/shard_map/adapter_attention/pallas_call | solution.py:359
  45.0 1.4 %copy.12 = bf16[1,1,64,128]{3,1,2,0:T(2,128)(2,1)} copy(bf16[1,1,64,128]{3,2,1,0:T(8,128)(2,1)} %bitcast.7) | data formatting | bytes 32768

commit v3 on v2

--- a/solution.py
+++ b/solution.py
@@ -164,6 +164,8 @@
         for k in range(1, chips):
             send_row(here, lax.rem(chip + k, chips) * 2 + core, k)
         send_row(here, sibling, 0)
+        while late:
+            late.pop().wait_send()
         for k in range(1, chips):
             p = core * chips + lax.rem(chip + chips - k, chips)
             arrived(p)
@@ -269,11 +271,13 @@
                 dev,
             )
             copy.start()
-            waits.append(copy)
+            late.append(copy)
         base_in[phase, pl.ds(pl.multiple_of(me * 8, 8), 8), :] = base_out[
             phase, pl.ds(pl.multiple_of(here * 8, 8), 8), :
         ]
 
+        for copy in waits:
+            copy.wait_send()
         totals = []
         for half in (0, 1):
             total = pair_delta[
@@ -297,10 +301,9 @@
         for src in range(n):
             row32[pl.ds(src * blocks, blocks), :] = base_in[phase, pl.ds(src * 8, blocks), :]
         result = (row32[...] + total).astype(BF16)
-        for copy in waits:
-            copy.wait_send()
         return result
 
+    late = []
     row32[...] = project(0).astype(F32)
 
     loaded("kv")
@@ -329,6 +332,8 @@
         )
 
     out_ref[...] = project(1)
+    for copy in late:
+        copy.wait_send()
 
 
 WPARTS = 4

time: 46.6 us -> 46.4 us (level)
  no operation moved by 1% of the time
where the time goes in v3:
time: 46.4 us; the launch traced here: 46.2 us
  Pallas kernels  44.2 us (95%)
  local copies, waits for them, and re-layouts  1.36 us (3%)
  between operations  0.66 us (1%)
    pallas_call x1, Pallas kernels, fused_body(): pl.pallas_call(functools.partial(attention_kernel, n), out_shape=jax.Shap...  44.2 us
    unnamed x1, local copies, waits for them, and re-layouts  1.36 us

profile of v3, /device:TPU:0, one launch (start us, length us, event | category | flops | bytes accessed | tf_op | source)
XLA Modules:
  0.0 46.2 jit_solution(2279562032735824320)
XLA Ops:
  0.7 44.2 %adapter_attention.1 = bf16[64,128]{1,0:T(8,128)(2,1)} custom-call(s32[16]{0:T(128)} %variant_hbm.1, s32[64]{0:T(128)} %slots_hbm.1, s32[1]{0:T(128)S(6)} %copy.13.length_hbm, bf16[1,8192]{1,0:T(2,128)(2,1)} %hidden_hbm.1, bf16[8192,512]{1,0:T(8,128)(2,1)} %wq_hbm.1, bf16[8192,512]{1,0:T(8,128)(2,1)} %wo_hbm.1, bf16[4,2,64,8192]{3,2,1,0:T(8,128)(2,1)} %bitcast.6, ...), custom_call_target="tpu_custom_call" | custom-call | flops 553648128 | bytes 35651584 | tf_op jit(solution)/shard_map/adapter_attention/pallas_call | solution.py:364
  44.8 1.4 %copy.12 = bf16[1,1,64,128]{3,1,2,0:T(2,128)(2,1)} copy(bf16[1,1,64,128]{3,2,1,0:T(8,128)(2,1)} %bitcast.7) | data formatting | bytes 32768

commit v4 on v3

--- a/solution.py
+++ b/solution.py
@@ -248,10 +248,10 @@
             )
 
         acc = jnp.zeros((n, cols), F32)
-        for part in range(WPARTS // 2):
+        for part in range(1):
             acc = base_part(part, acc)
         forward(1)
-        for part in range(WPARTS // 2, WPARTS):
+        for part in range(1, WPARTS):
             acc = base_part(part, acc)
         acc = acc.astype(BF16).astype(F32)
         for j in range(blocks):

time: 46.4 us -> 47.3 us (1.019)
  Pallas kernels: 44.2 us -> 45 us
    pallas_call x1, Pallas kernels: 44.2 us -> 45 us  [fused_body(): pl.pallas_call(functools.partial(attention_kernel, n), out_shape=jax.Shap...]
where the time goes in v4:
time: 47.3 us; the launch traced here: 47.1 us
  Pallas kernels  45 us (95%)
  local copies, waits for them, and re-layouts  1.36 us (3%)
  between operations  0.66 us (1%)
    pallas_call x1, Pallas kernels, fused_body(): pl.pallas_call(functools.partial(attention_kernel, n), out_shape=jax.Shap...  45 us
    unnamed x1, local copies, waits for them, and re-layouts  1.36 us

profile of v4, /device:TPU:0, one launch (start us, length us, event | category | flops | bytes accessed | tf_op | source)
XLA Modules:
  0.0 47.1 jit_solution(3477342244619833992)
XLA Ops:
  0.7 45.0 %adapter_attention.1 = bf16[64,128]{1,0:T(8,128)(2,1)} custom-call(s32[16]{0:T(128)} %variant_hbm.1, s32[64]{0:T(128)} %slots_hbm.1, s32[1]{0:T(128)S(6)} %copy.13.length_hbm, bf16[1,8192]{1,0:T(2,128)(2,1)} %hidden_hbm.1, bf16[8192,512]{1,0:T(8,128)(2,1)} %wq_hbm.1, bf16[8192,512]{1,0:T(8,128)(2,1)} %wo_hbm.1, bf16[4,2,64,8192]{3,2,1,0:T(8,128)(2,1)} %bitcast.6, ...), custom_call_target="tpu_custom_call" | custom-call | flops 553648128 | bytes 35651584 | tf_op jit(solution)/shard_map/adapter_attention/pallas_call | solution.py:364
  45.7 1.4 %copy.12 = bf16[1,1,64,128]{3,1,2,0:T(2,128)(2,1)} copy(bf16[1,1,64,128]{3,2,1,0:T(8,128)(2,1)} %bitcast.7) | data formatting | bytes 32768
